TPU v7x, 32 devices: a whole 2x2x4 slice. The times are simulated.
32 devices in a mesh: groups: 2 (over y), tm: 16 (over z, x, core), rows: 1.
Axes of the slice: x: 2, y: 2, z: 4, core: 2. Of those that a mesh axis runs over, the one named last changes fastest.
Arguments:
- queries: bfloat16 [32, 4, 64, 1024], P(('groups', 'tm'), 'rows'), parts along dimension 0, may hold values from -60 to 60
- keys: bfloat16 [32, 4, 64, 256], P(('groups', 'tm'), 'rows'), parts along dimension 0, may hold values from -4 to 4
- values: bfloat16 [32, 4, 64, 256], P(('groups', 'tm'), 'rows'), parts along dimension 0, may hold values from -6 to 6
- grad_out: bfloat16 [32, 4, 64, 1024], P(('groups', 'tm'), 'rows'), parts along dimension 0, may hold values from -12 to 12
- frame_mask: int32 [32, 16], P('groups'), parts along dimension 0, may hold values 0 or 1
- clip_frames: int32 [12], P('groups'), parts along dimension 0, may hold values from 1 to 4, 16 in all
- offsets: int32 [24, 2], replicated, may hold values from -3 to 3, as said below
Outputs:
- grad_queries: float32 [32, 4, 64, 1024], P(('groups', 'tm'), 'rows'), parts along dimension 0
- grad_keys: float32 [32, 4, 64, 256], P(('groups', 'tm'), 'rows'), parts along dimension 0
- grad_values: float32 [32, 4, 64, 256], P(('groups', 'tm'), 'rows'), parts along dimension 0
There are 2 independent parts, one for each index of `groups`. A program takes and returns all parts, laid end to end along the dimension named above; an argument that names none is the same for every part. Nothing has to cross between parts.
Inputs may be any that keep to these rules, and one draw needn't show every extreme that they name: `offsets`: row 0 is (0, 0) and row 1 is (0, 1); the rows are distinct cells of the 7 x 7 neighbourhood. `clip_frames`: the lengths sum to 16; the longest clip has exactly 4 frames.
All inputs are finite; a program needn't handle non-finite values.
Results may differ from a plain program's by a relative error of at most 0.005.
Values may be sent and summed in bfloat16 or wider, within the bound.
A program may use at most 128 MiB of HBM per device.

v0:
```python
import jax
import jax.numpy as jnp
from jax import lax
from jax.experimental import pallas as pl
from jax.experimental.pallas import tpu as pltpu
from jax.sharding import PartitionSpec as P

HQ = 8
HK = 2
HD = 128


tile_cols = 8
key_span = 14
negative_big = -1e30


def padded_2(cells, sides, width):
    for axis, dim in sides:
        count = lax.axis_size(axis)
        ends = count - 1
        head = lax.slice_in_dim(cells, 0, width, axis=dim)
        tail = lax.slice_in_dim(cells, cells.shape[dim] - width, cells.shape[dim], axis=dim)
        cells = jnp.concatenate(
            [
                lax.ppermute(tail, axis, [(i, (i + 1) % count) for i in range(ends)]),
                cells,
                lax.ppermute(head, axis, [((i + 1) % count, i) for i in range(ends)]),
            ],
            axis=dim,
        )
    return cells


def passed_along(value, axis, steps):
    count = lax.axis_size(axis)
    pairs = [(source, (source + steps) % count) for source in range(count)]
    return lax.ppermute(value, axis, pairs)


def to_tiles(block, group_size):
    band_rows = block.shape[0]
    count_tiles = block.shape[1] // tile_cols
    shaped = block.reshape(band_rows, count_tiles, tile_cols, HK, group_size, HD)
    shaped = shaped.transpose(1, 3, 4, 0, 2, 5)
    return shaped.reshape(count_tiles, HK, group_size, band_rows * tile_cols, HD)


def from_tiles(tiles, band_rows):
    count_tiles = tiles.shape[0]
    group_size = tiles.shape[2]
    shaped = tiles.reshape(count_tiles, HK, group_size, band_rows, tile_cols, HD)
    shaped = shaped.transpose(3, 0, 4, 1, 2, 5)
    return shaped.reshape(1, band_rows, count_tiles * tile_cols, HK * group_size * HD)


def to_windows(extended):
    ext_rows = extended.shape[1]
    total_width = extended.shape[2]
    padded = jnp.pad(extended, ((0, 0), (0, 0), (3, 3), (0, 0)))
    pieces = [
        padded[:, :, column_tile * tile_cols : column_tile * tile_cols + key_span]
        for column_tile in range(total_width // tile_cols)
    ]
    stacked = jnp.stack(pieces, 0)
    stacked = stacked.reshape(len(pieces), 2, ext_rows, key_span, HK, HD)
    stacked = stacked.transpose(1, 0, 4, 2, 3, 5)
    return stacked.reshape(2, len(pieces), HK, ext_rows * key_span, HD)


def from_windows(window_grads, ext_rows, total_width):
    count_tiles = window_grads.shape[1]
    shaped = window_grads.reshape(2, count_tiles, HK, ext_rows, key_span, HD)
    shaped = shaped.transpose(0, 1, 3, 4, 2, 5).reshape(2, count_tiles, ext_rows, key_span, HK * HD)
    summed = jnp.zeros((2, ext_rows, total_width + 6, HK * HD), jnp.float32)
    for column_tile in range(count_tiles):
        first_col = column_tile * tile_cols
        summed = summed.at[:, :, first_col : first_col + key_span].add(shaped[:, column_tile])
    return summed[:, :, 3 : 3 + total_width]


def spatial_live(offsets, band_rows, total_width):
    ext_rows = band_rows + 6
    count_tiles = total_width // tile_cols
    query_row = jnp.repeat(jnp.arange(band_rows), tile_cols)
    query_col = jnp.tile(jnp.arange(tile_cols), band_rows)
    key_row = jnp.repeat(jnp.arange(ext_rows), key_span)
    key_col = jnp.tile(jnp.arange(key_span), ext_rows)
    delta_row = key_row[None, :] - 3 - query_row[:, None]
    delta_col = key_col[None, :] - 3 - query_col[:, None]
    offset_hit = jnp.any(
        (delta_row[None] == offsets[:, 0, None, None])
        & (delta_col[None] == offsets[:, 1, None, None]),
        axis=0,
    )
    band_index = lax.axis_index("rows")
    image_rows = band_rows * lax.axis_size("rows")
    image_row = band_index * band_rows + key_row - 3
    row_inside = (image_row >= 0) & (image_row < image_rows)
    tile_first = jnp.arange(count_tiles) * tile_cols
    image_col = tile_first[:, None] + key_col[None, :] - 3
    col_inside = (image_col >= 0) & (image_col < total_width)
    return offset_hit[None] & row_inside[None, None] & col_inside[:, None, :]


def running_sum(entries):
    places = jnp.arange(entries.shape[0])
    return jnp.sum(jnp.where(places[None, :] <= places[:, None], entries[None, :], 0), axis=1)


def frame_allowed(frame_mask, clip_frames, distance):
    frames = lax.axis_size("tm")
    lags = min(4, frames)
    own_frame = lax.axis_index("tm")
    seen_frame = (own_frame - distance) % frames
    clip_ends = running_sum(clip_frames)
    clip_starts = clip_ends - clip_frames
    is_longest = (clip_frames == lags).astype(jnp.int32)
    first_longest = (is_longest == 1) & (running_sum(is_longest) == 1)
    rotation = jnp.sum(jnp.where(first_longest, clip_starts, 0))
    own_place = (own_frame + 2 + rotation) % frames
    seen_place = (seen_frame + 2 + rotation) % frames
    own_clip = jnp.sum((own_place >= clip_ends).astype(jnp.int32))
    seen_clip = jnp.sum((seen_place >= clip_ends).astype(jnp.int32))
    grid_rows = jnp.arange(frames)[:, None]
    grid_cols = jnp.arange(frames)[None, :]
    picked = jnp.sum(jnp.where((grid_rows == own_frame) & (grid_cols == seen_frame), frame_mask, 0))
    kept = (picked == 1) | (distance <= 1)
    return (own_clip == seen_clip) & (seen_place <= own_place) & kept


def fold_rims(extended_grads, band_rows):
    interior = extended_grads[:, 3 : 3 + band_rows]
    rim_rows = jnp.concatenate([extended_grads[:, :3], extended_grads[:, band_rows + 3 :]], 1)
    haloed = padded_2(rim_rows.astype(jnp.bfloat16), (("rows", 1),), 3).astype(rim_rows.dtype)
    interior = interior.at[:, :3].add(haloed[:, :3])
    return interior.at[:, band_rows - 3 :].add(haloed[:, 9:])


def body(queries, keys, values, grad_out, frame_mask, clip_frames, offsets):
    band_rows = queries.shape[1]
    total_width = queries.shape[2]
    ext_rows = band_rows + 6
    group_size = HQ // HK
    scale = HD ** (-0.5)
    lags = min(4, lax.axis_size("tm"))
    query_tiles = to_tiles(queries[0], group_size)
    grad_tiles = to_tiles(grad_out[0], group_size)
    spatial = spatial_live(offsets, band_rows, total_width)[:, None, None]
    allowed = [frame_allowed(frame_mask, clip_frames, distance) for distance in range(lags)]
    stacked = jnp.stack([keys[0], values[0]], 0)
    resident = padded_2(stacked, (("rows", 1),), 3)

    def pair_terms(extended):
        windows = to_windows(extended)
        logits = (
            jnp.einsum(
                "cgaqd,cgkd->cgaqk", query_tiles, windows[0], preferred_element_type=jnp.float32
            )
            * scale
        )
        grad_dot = jnp.einsum(
            "cgaqd,cgkd->cgaqk", grad_tiles, windows[1], preferred_element_type=jnp.float32
        )
        return (windows, logits, grad_dot)

    stat_shape = (total_width // tile_cols, HK, group_size, band_rows * tile_cols)
    running = (
        jnp.full(stat_shape, negative_big, jnp.float32),
        jnp.zeros(stat_shape, jnp.float32),
        jnp.zeros(stat_shape, jnp.float32),
    )
    visiting = resident
    visited = []
    for distance in range(lags):
        visited.append(visiting)
        extended = visiting
        live_mask = spatial & allowed[distance]
        run_max, run_sum, run_dot = running
        stat_windows, stat_logits, stat_grad_dot = pair_terms(extended)
        masked = jnp.where(live_mask, stat_logits, negative_big)
        new_max = jnp.maximum(run_max, jnp.max(masked, axis=-1))
        factor = jnp.exp(run_max - new_max)
        weights = jnp.where(live_mask, jnp.exp(stat_logits - new_max[..., None]), 0.0)
        running = (
            new_max,
            run_sum * factor + jnp.sum(weights, axis=-1),
            run_dot * factor + jnp.sum(weights * stat_grad_dot, axis=-1),
        )
        if distance + 1 < lags:
            visiting = passed_along(visiting, "tm", 1)
    log_total = running[0] + jnp.log(running[1])
    mean_grad = running[2] / running[1]
    query_total = jnp.zeros(stat_shape + (HD,), jnp.float32)
    carried = jnp.zeros(resident.shape, jnp.float32)
    visiting = resident
    for distance in range(lags):
        extended = visiting
        live_mask = spatial & allowed[distance]
        grad_windows, grad_logits, grad_grad_dot = pair_terms(extended)
        probs = jnp.where(live_mask, jnp.exp(grad_logits - log_total[..., None]), 0.0)
        probs_low = probs.astype(jnp.bfloat16)
        dscore = (probs * (grad_grad_dot - mean_grad[..., None])).astype(jnp.bfloat16)
        query_part = jnp.einsum(
            "cgaqk,cgkd->cgaqd", dscore, grad_windows[0], preferred_element_type=jnp.float32
        )
        key_part = (
            jnp.einsum("cgaqk,cgaqd->cgkd", dscore, query_tiles, preferred_element_type=jnp.float32)
            * scale
        )
        value_part = jnp.einsum(
            "cgaqk,cgaqd->cgkd", probs_low, grad_tiles, preferred_element_type=jnp.float32
        )
        query_part, window_grads = (query_part, jnp.stack([key_part, value_part], 0))
        query_total = query_total + query_part
        ext_grads = from_windows(window_grads, ext_rows, total_width)
        carried = carried + ext_grads
        if distance + 1 < lags:
            visiting = passed_along(visiting, "tm", 1)
            carried = passed_along(carried, "tm", 1)
    carried = passed_along(carried, "tm", 1 - lags)
    finished = fold_rims(carried, band_rows)
    grad_queries = from_tiles(query_total * scale, band_rows)
    return (grad_queries, finished[0][None], finished[1][None])


MESH = pl.DeviceIdType.MESH
LOG2E = 1.4426950408889634
SCALE = HD**-0.5
GROUP = HQ // HK


def lag_allowed(mask_ref, clip_ref, own_frame, frames, lag):
    clips = clip_ref.shape[0]
    seen_frame = lax.rem(own_frame - lag + frames, frames)
    total = jnp.int32(0)
    rotation = jnp.int32(0)
    found = jnp.int32(0)
    for clip in range(clips):
        length = clip_ref[clip]
        first = jnp.where(length == 4, 1, 0) * (1 - found)
        rotation = rotation + first * total
        found = found + first
        total = total + length
    own_place = own_frame + 2 + rotation
    own_place = jnp.where(own_place >= frames, own_place - frames, own_place)
    own_place = jnp.where(own_place >= frames, own_place - frames, own_place)
    seen_place = seen_frame + 2 + rotation
    seen_place = jnp.where(seen_place >= frames, seen_place - frames, seen_place)
    seen_place = jnp.where(seen_place >= frames, seen_place - frames, seen_place)
    own_clip = jnp.int32(0)
    seen_clip = jnp.int32(0)
    end = jnp.int32(0)
    for clip in range(clips):
        end = end + clip_ref[clip]
        own_clip = own_clip + jnp.where(own_place >= end, 1, 0)
        seen_clip = seen_clip + jnp.where(seen_place >= end, 1, 0)
    kept = jnp.maximum(jnp.where(mask_ref[own_frame, seen_frame] == 1, 1, 0), jnp.where(lag <= 1, 1, 0))
    same = jnp.where(own_clip == seen_clip, 1, 0)
    causal = jnp.where(seen_place <= own_place, 1, 0)
    return kept * same * causal


def fused(
    width, frames,
    mask_hbm, clip_hbm, offset_hbm, query_hbm, key_hbm, value_hbm, cot_hbm,
    dq_hbm, kv_grads_ref,
    dq_ref, mask_ref, clip_ref, offset_ref, query_ref, cot_ref, kv, grads, arrived, bias, probs, dots, tops, sums, means, dq_acc, load_sem, send_sem, recv_sem,
):
    tokens = query_ref.shape[0]
    heads_wide = HK * HD
    pairs = (
        (key_hbm, kv.at[0, :, pl.ds(0, heads_wide)]),
        (value_hbm, kv.at[0, :, pl.ds(heads_wide, heads_wide)]),
        (offset_hbm, offset_ref),
        (clip_hbm, clip_ref),
        (mask_hbm, mask_ref),
        (query_hbm, query_ref),
        (cot_hbm, cot_ref),
    )
    loads = [pltpu.make_async_copy(pair[0], pair[1], load_sem.at[i]) for i, pair in enumerate(pairs)]
    for load in loads:
        load.start()
    own = lax.axis_index("tm")
    core = lax.rem(own, 2)

    def device(step):
        return {"tm": lax.rem(own + step + frames, frames)}

    partner = device(1 - 2 * core)
    ahead, behind = device(2), device(frames - 2)
    far = device(jnp.where(core == 0, frames - 3, 3))
    second_to = device(jnp.where(core == 0, 1, 3))
    second_back = device(jnp.where(core == 0, frames - 3, frames - 1))

    barrier = pltpu.get_barrier_semaphore()
    for peer in (partner, ahead, behind, far):
        pl.semaphore_signal(barrier, inc=1, device_id=peer, device_id_type=MESH)
    for load in loads[:2]:
        load.wait()
    pl.semaphore_wait(barrier, 4)

    def remote(index, source, target, peer):
        return pltpu.make_async_remote_copy(
            src_ref=source, dst_ref=target, send_sem=send_sem.at[index], recv_sem=recv_sem.at[index],
            device_id=peer, device_id_type=MESH,
        )

    send_two = remote(0, kv.at[0], kv.at[2], ahead)
    send_one = remote(1, kv.at[0], kv.at[1], second_to)
    relay = remote(2, kv.at[2], kv.at[3], partner)
    send_two.start()
    for load in loads[2:]:
        load.wait()

    key_id = lax.broadcasted_iota(jnp.int32, (tokens, tokens), 0)
    query_id = lax.broadcasted_iota(jnp.int32, (tokens, tokens), 1)
    delta_col = lax.rem(key_id, width) - lax.rem(query_id, width)
    delta_row = key_id // width - query_id // width
    code = jnp.where((delta_col >= -3) & (delta_col <= 3), delta_row * 8 + delta_col, 1000)

    def mark(index, hit):
        wanted = offset_ref[0, index] * 8 + offset_ref[1, index]
        return jnp.where(code == wanted, 0.0, hit)

    bias[...] = lax.fori_loop(
        0, offset_ref.shape[1], mark, jnp.full((tokens, tokens), negative_big, jnp.float32), unroll=True
    )

    def lanes(index):
        return pl.ds(pl.multiple_of(index * HD, HD), HD)

    def scores(role, lag):
        allow = lag_allowed(mask_ref, clip_ref, own, frames, lag)
        shut = jnp.where(allow == 1, 0.0, negative_big).astype(jnp.float32)

        def head(h, _):
            group = h // GROUP
            key = kv[role, :, lanes(group)]
            value = kv[role, :, lanes(HK + group)]
            logit = lax.dot_general(
                key, query_ref[:, lanes(h)], (((1,), (1,)), ((), ())), preferred_element_type=jnp.float32
            )
            dot = lax.dot_general(
                value, cot_ref[:, lanes(h)], (((1,), (1,)), ((), ())), preferred_element_type=jnp.float32
            )
            logit = logit * (SCALE * LOG2E) + (bias[...] + shut)
            top = jnp.max(logit, axis=0, keepdims=True)
            weight = jnp.exp2(logit - top)
            probs[role, h] = weight
            dots[role, h] = dot
            tops[role, h] = top
            sums[role, h] = jnp.sum(weight, axis=0, keepdims=True)
            means[role, h] = jnp.sum(weight * dot, axis=0, keepdims=True)
            return 0

        lax.fori_loop(0, HQ, head, 0, unroll=4)

    lag_second = jnp.where(core == 0, 3, 1)
    lag_relay = jnp.where(core == 0, 1, 3)
    scores(0, jnp.int32(0))
    send_two.wait_send()
    send_one.start()
    send_two.wait_recv()
    relay.start()
    scores(2, jnp.int32(2))
    relay.wait_recv()
    scores(3, lag_relay)
    send_one.wait_recv()
    scores(1, lag_second)

    def finish(h, _):
        top = jnp.maximum(jnp.maximum(tops[0, h], tops[1, h]), jnp.maximum(tops[2, h], tops[3, h]))
        factors = [jnp.exp2(tops[role, h] - top) for role in range(4)]
        total = sum(factors[role] * sums[role, h] for role in range(4))
        dot = sum(factors[role] * means[role, h] for role in range(4))
        for role in range(4):
            tops[role, h] = factors[role] / total
        means[0, h] = dot / total
        return 0

    lax.fori_loop(0, HQ, finish, 0)

    def gradients(role, first, store):
        def one_group(group, _):
            key_turned = kv[role, :, lanes(group)].T
            key_sum = None
            value_sum = None
            for a in range(GROUP):
                h = group * GROUP + a
                prob = probs[role, h] * tops[role, h]
                score = (prob * (dots[role, h] - means[0, h])).astype(jnp.bfloat16)
                key_part = jnp.dot(score, query_ref[:, lanes(h)], preferred_element_type=jnp.float32)
                value_part = jnp.dot(
                    prob.astype(jnp.bfloat16), cot_ref[:, lanes(h)], preferred_element_type=jnp.float32
                )
                turned = jnp.dot(key_turned, score, preferred_element_type=jnp.float32)
                key_sum = key_part if a == 0 else key_sum + key_part
                value_sum = value_part if a == 0 else value_sum + value_part
                dq_acc[h] = turned if first else dq_acc[h] + turned
            store(group, key_sum * SCALE, value_sum)
            return 0

        lax.fori_loop(0, HK, one_group, 0)

    def store_out(role):
        def store(group, key_sum, value_sum):
            grads[role, :, lanes(group)] = key_sum.astype(jnp.bfloat16)
            grads[role, :, lanes(HK + group)] = value_sum.astype(jnp.bfloat16)

        return store

    back_relay = remote(3, grads.at[2], arrived.at[2], partner)
    back_two = remote(4, grads.at[1], arrived.at[1], behind)
    back_one = remote(5, grads.at[0], arrived.at[0], second_back)
    gradients(3, True, store_out(2))
    back_relay.start()
    gradients(1, False, store_out(0))
    back_one.start()

    def store_two(group, key_sum, value_sum):
        grads[1, :, lanes(group)] = key_sum.astype(jnp.bfloat16)
        grads[1, :, lanes(HK + group)] = value_sum.astype(jnp.bfloat16)

    gradients(2, False, store_two)
    back_relay.wait_recv()
    grads[1] = (grads[1].astype(jnp.float32) + arrived[2].astype(jnp.float32)).astype(jnp.bfloat16)
    back_two.start()

    def store_own(group, key_sum, value_sum):
        kv_grads_ref[0, :, lanes(group)] = key_sum
        kv_grads_ref[1, :, lanes(group)] = value_sum

    gradients(0, False, store_own)

    def query_out(h, _):
        dq_ref[:, lanes(h)] = dq_acc[h].T * SCALE
        return 0

    lax.fori_loop(0, HQ, query_out, 0, unroll=4)
    store_queries = pltpu.make_async_copy(dq_ref, dq_hbm, load_sem.at[7])
    store_queries.start()
    back_two.wait_recv()
    back_one.wait_recv()
    came = arrived[0].astype(jnp.float32) + arrived[1].astype(jnp.float32)
    kv_grads_ref[0] = kv_grads_ref[0] + came[:, :heads_wide]
    kv_grads_ref[1] = kv_grads_ref[1] + came[:, heads_wide:]
    for copy in (send_one, relay, back_relay, back_two, back_one):
        copy.wait_send()
    store_queries.wait()


def fused_body(queries, keys, values, grad_out, frame_mask, clip_frames, offsets):
    _, rows, width, wide = queries.shape
    tokens = rows * width
    narrow = keys.shape[3]
    frames = lax.axis_size("tm")

    def flat(array):
        return array.reshape(tokens, array.shape[3])

    hbm = pl.BlockSpec(memory_space=pltpu.HBM)
    vmem = pl.BlockSpec(memory_space=pltpu.VMEM)

    def kernel(*refs):
        fused(width, frames, *refs)

    dq, kv_grads = pl.pallas_call(
        kernel,
        out_shape=(
            jax.ShapeDtypeStruct((tokens, wide), jnp.float32),
            jax.ShapeDtypeStruct((2, tokens, narrow), jnp.float32),
        ),
        in_specs=[hbm] * 7,
        out_specs=(hbm, vmem),
        scratch_shapes=[
            pltpu.VMEM((tokens, wide), jnp.float32),
            pltpu.SMEM(frame_mask.shape, jnp.int32),
            pltpu.SMEM(clip_frames.shape, jnp.int32),
            pltpu.SMEM(offsets.shape[::-1], jnp.int32),
            pltpu.VMEM((tokens, wide), jnp.bfloat16),
            pltpu.VMEM((tokens, wide), jnp.bfloat16),
            pltpu.VMEM((4, tokens, 2 * narrow), jnp.bfloat16),
            pltpu.VMEM((3, tokens, 2 * narrow), jnp.bfloat16),
            pltpu.VMEM((3, tokens, 2 * narrow), jnp.bfloat16),
            pltpu.VMEM((tokens, tokens), jnp.float32),
            pltpu.VMEM((4, HQ, tokens, tokens), jnp.float32),
            pltpu.VMEM((4, HQ, tokens, tokens), jnp.float32),
            pltpu.VMEM((4, HQ, 1, tokens), jnp.float32),
            pltpu.VMEM((4, HQ, 1, tokens), jnp.float32),
            pltpu.VMEM((4, HQ, 1, tokens), jnp.float32),
            pltpu.VMEM((HQ, HD, tokens), jnp.float32),
            pltpu.SemaphoreType.DMA((8,)),
            pltpu.SemaphoreType.DMA((6,)),
            pltpu.SemaphoreType.DMA((6,)),
        ],
        compiler_params=pltpu.CompilerParams(
            collective_id=0, has_side_effects=True, vmem_limit_bytes=63 * 1024 * 1024 - 65536
        ),
    )(frame_mask, clip_frames, offsets.T, flat(queries), flat(keys), flat(values), flat(grad_out))
    shape = (1, rows, width)
    return dq.reshape(shape + (wide,)), kv_grads[0].reshape(shape + (narrow,)), kv_grads[1].reshape(shape + (narrow,))


def solution(mesh):
    whole_rows = mesh.shape["rows"] == 1 and mesh.shape["tm"] % 2 == 0 and mesh.shape["tm"] > 6
    return jax.shard_map(
        fused_body if whole_rows else body,
        mesh=mesh,
        in_specs=(
            P(("groups", "tm"), "rows", None, None),
            P(("groups", "tm"), "rows", None, None),
            P(("groups", "tm"), "rows", None, None),
            P(("groups", "tm"), "rows", None, None),
            P("groups", None),
            P("groups"),
            P(),
        ),
        out_specs=(
            P(("groups", "tm"), "rows", None, None),
            P(("groups", "tm"), "rows", None, None),
            P(("groups", "tm"), "rows", None, None),
        ),
        check_vma=False,
    )
```

profile of v0, /device:TPU:0, one launch (start us, length us, event | category | flops | bytes accessed | tf_op | source)
XLA Modules:
  0.0 33.8 jit_solution(7661722882343705082)
XLA Ops:
  0.6 30.2 %shard_map.94 = (f32[256,1024]{1,0:T(8,128)}, f32[2,256,256]{2,1,0:T(8,128)}) custom-call(s32[16,16]{1,0:T(8,128)} %refs_0_.1, s32[6]{0:T(128)} %refs_1_.1, s32[2,24]{1,0:T(2,128)} %bitcast.15, bf16[256,1024]{1,0:T(8,128)(2,1)} %bitcast.9, bf16[256,256]{1,0:T(8,128)(2,1)} %bitcast.13, bf16[256,256]{1,0:T(8,128)(2,1)} %bitcast.14, bf16[256,1024]{1,0:T(8,128)(2,1)} %bitcast.10), custom_call_target="tpu_custom_call" | custom-call | tf_op jit(solution)/shard_map/pallas_call | solution.py:468
  30.9 0.0 copy-start
  30.9 1.9 %fusion = (f32[1,256,256]{2,1,0:T(8,128)}, f32[1,256,256]{2,1,0:T(8,128)}) fusion(f32[2,256,256]{2,1,0:T(8,128)} %get-tuple-element.6), kind=kLoop, calls=%fused_computation | loop fusion | bytes 1048576 | tf_op jit(solution)/shard_map/slice | solution.py:502
  32.8 0.0 copy-done
  32.8 1.0 %copy.11 = f32[1,4,64,1024]{3,2,1,0:T(8,128)} copy(f32[1,4,64,1024]{3,2,1,0:T(8,128)S(1)} %bitcast.8) | data formatting | bytes 2097152
Async XLA Ops:
  30.9 2.0 %copy-start = (f32[256,1024]{1,0:T(8,128)S(1)}, f32[256,1024]{1,0:T(8,128)}, u32[]{:S(2)}) copy-start(f32[256,1024]{1,0:T(8,128)} %get-tuple-element.5) | copy-start | bytes 3145732
where the time goes:
time: 33.9 us; the launch traced here: 33.8 us
  Pallas kernels  30.2 us (89%)
  local copies, waits for them, and re-layouts  2.91 us (9%)
  between operations  0.65 us (2%)
    pallas_call x1, Pallas kernels, fused_body(): pl.pallas_call(kernel, out_shape=(jax.ShapeDtypeStruct((tokens, wide), jn...  30.2 us
    slice x1, local copies, waits for them, and re-layouts, fused_body(): kv_grads[1].reshape(shape + (narrow,))  1.94 us
    unnamed x3, local copies, waits for them, and re-layouts  0.97 us

commit v1 on v0

--- a/solution.py
+++ b/solution.py
@@ -261,44 +261,56 @@
     return kept * same * causal
 
 
+TILE = 8
+REACH = 4
+
+
 def fused(
     width, frames,
     mask_hbm, clip_hbm, offset_hbm, query_hbm, key_hbm, value_hbm, cot_hbm,
-    dq_hbm, kv_grads_ref,
-    dq_ref, mask_ref, clip_ref, offset_ref, query_ref, cot_ref, kv, grads, arrived, bias, probs, dots, tops, sums, means, dq_acc, load_sem, send_sem, recv_sem,
+    dq_out, dk_out, dv_out,
+    mask_ref, clip_ref, offset_ref, query_ref, cot_ref, raw, keyed, mixed, bias, held, own_grads, grads, arrived,
+    scores_low, dq_acc, final, load_sem, send_sem, recv_sem,
 ):
     tokens = query_ref.shape[0]
-    heads_wide = HK * HD
-    pairs = (
-        (key_hbm, kv.at[0, :, pl.ds(0, heads_wide)]),
-        (value_hbm, kv.at[0, :, pl.ds(heads_wide, heads_wide)]),
+    rows = tokens // width
+    tiles = width // TILE
+    tile = TILE * rows
+    rim = REACH * rows
+    span = tile + 2 * rim
+    lane_count = GROUP * tile
+
+    def lanes(index):
+        return pl.ds(pl.multiple_of(index * HD, HD), HD)
+
+    pairs = [
         (offset_hbm, offset_ref),
         (clip_hbm, clip_ref),
         (mask_hbm, mask_ref),
         (query_hbm, query_ref),
         (cot_hbm, cot_ref),
-    )
+    ]
+    for g in range(HK):
+        pairs.append((key_hbm.at[:, lanes(g)], raw.at[0, g, :, pl.ds(0, HD)]))
+        pairs.append((value_hbm.at[:, lanes(g)], raw.at[0, g, :, pl.ds(HD, HD)]))
     loads = [pltpu.make_async_copy(pair[0], pair[1], load_sem.at[i]) for i, pair in enumerate(pairs)]
+    own = lax.axis_index("tm")
+    core = lax.rem(own, 2)
+
+    def device(step):
+        return {"tm": lax.rem(own + step + frames, frames)}
+
+    partner = device(1 - 2 * core)
+    ahead, behind = device(2), device(frames - 2)
+    third = device(jnp.where(core == 0, frames - 3, frames - 1))
+    second_to = device(jnp.where(core == 0, 1, 3))
+    second_back = device(jnp.where(core == 0, frames - 3, frames - 1))
+
+    barrier = pltpu.get_barrier_semaphore()
+    for peer in (partner, behind, third):
+        pl.semaphore_signal(barrier, inc=1, device_id=peer, device_id_type=MESH)
     for load in loads:
         load.start()
-    own = lax.axis_index("tm")
-    core = lax.rem(own, 2)
-
-    def device(step):
-        return {"tm": lax.rem(own + step + frames, frames)}
-
-    partner = device(1 - 2 * core)
-    ahead, behind = device(2), device(frames - 2)
-    far = device(jnp.where(core == 0, frames - 3, 3))
-    second_to = device(jnp.where(core == 0, 1, 3))
-    second_back = device(jnp.where(core == 0, frames - 3, frames - 1))
-
-    barrier = pltpu.get_barrier_semaphore()
-    for peer in (partner, ahead, behind, far):
-        pl.semaphore_signal(barrier, inc=1, device_id=peer, device_id_type=MESH)
-    for load in loads[:2]:
-        load.wait()
-    pl.semaphore_wait(barrier, 4)
 
     def remote(index, source, target, peer):
         return pltpu.make_async_remote_copy(
@@ -306,148 +318,169 @@
             device_id=peer, device_id_type=MESH,
         )
 
-    send_two = remote(0, kv.at[0], kv.at[2], ahead)
-    send_one = remote(1, kv.at[0], kv.at[1], second_to)
-    relay = remote(2, kv.at[2], kv.at[3], partner)
-    send_two.start()
-    for load in loads[2:]:
+    def outward(slot, role, g, peer):
+        return (
+            remote(slot, key_hbm.at[:, lanes(g)], raw.at[role, g, :, pl.ds(0, HD)], peer),
+            remote(slot + 1, value_hbm.at[:, lanes(g)], raw.at[role, g, :, pl.ds(HD, HD)], peer),
+        )
+
+    send_two = [outward(2 * g, 2, g, ahead) for g in range(HK)]
+    send_one = [outward(4 + 2 * g, 1, g, second_to) for g in range(HK)]
+    relay = [remote(8 + g, raw.at[2, g], raw.at[3, g], partner) for g in range(HK)]
+    inner = pl.ds(rim, tokens)
+    back_relay = [remote(10 + g, grads.at[2, g, inner], arrived.at[2, g], partner) for g in range(HK)]
+    back_two = [remote(12 + g, grads.at[1, g, inner], arrived.at[1, g], behind) for g in range(HK)]
+    back_one = [remote(14 + g, grads.at[0, g, inner], arrived.at[0, g], second_back) for g in range(HK)]
+
+    pl.semaphore_wait(barrier, 3)
+    for g in range(HK):
+        for copy in send_two[g] + send_one[g]:
+            copy.start()
+
+    new_id = lax.broadcasted_iota(jnp.int32, (tokens, tokens), 0)
+    old_id = lax.broadcasted_iota(jnp.int32, (tokens, tokens), 1)
+    turn = jnp.where((new_id % rows) * width + new_id // rows == old_id, 1.0, 0.0).astype(jnp.bfloat16)
+
+    def permuted(block):
+        return jnp.dot(turn, block, preferred_element_type=jnp.float32).astype(jnp.bfloat16)
+
+    for load in loads[:3]:
         load.wait()
-
-    key_id = lax.broadcasted_iota(jnp.int32, (tokens, tokens), 0)
-    query_id = lax.broadcasted_iota(jnp.int32, (tokens, tokens), 1)
-    delta_col = lax.rem(key_id, width) - lax.rem(query_id, width)
-    delta_row = key_id // width - query_id // width
+    key_id = lax.broadcasted_iota(jnp.int32, (span, lane_count), 0)
+    query_id = lax.broadcasted_iota(jnp.int32, (span, lane_count), 1) % tile
+    delta_row = key_id % rows - query_id % rows
+    delta_col = key_id // rows - REACH - query_id // rows
     code = jnp.where((delta_col >= -3) & (delta_col <= 3), delta_row * 8 + delta_col, 1000)
 
     def mark(index, hit):
         wanted = offset_ref[0, index] * 8 + offset_ref[1, index]
         return jnp.where(code == wanted, 0.0, hit)
 
-    bias[...] = lax.fori_loop(
-        0, offset_ref.shape[1], mark, jnp.full((tokens, tokens), negative_big, jnp.float32), unroll=True
+    spatial = lax.fori_loop(
+        0, offset_ref.shape[1], mark, jnp.full((span, lane_count), negative_big, jnp.float32), unroll=True
     )
-
-    def lanes(index):
-        return pl.ds(pl.multiple_of(index * HD, HD), HD)
-
-    def scores(role, lag):
-        allow = lag_allowed(mask_ref, clip_ref, own, frames, lag)
+    lags = (jnp.int32(0), jnp.where(core == 0, 3, 1), jnp.int32(2), jnp.where(core == 0, 1, 3))
+    for role in range(4):
+        allow = lag_allowed(mask_ref, clip_ref, own, frames, lags[role])
         shut = jnp.where(allow == 1, 0.0, negative_big).astype(jnp.float32)
-
-        def head(h, _):
-            group = h // GROUP
-            key = kv[role, :, lanes(group)]
-            value = kv[role, :, lanes(HK + group)]
-            logit = lax.dot_general(
-                key, query_ref[:, lanes(h)], (((1,), (1,)), ((), ())), preferred_element_type=jnp.float32
+        bias[1, role] = spatial + shut
+        bias[0, role] = jnp.where(key_id < rim, negative_big, spatial) + shut
+        bias[2, role] = jnp.where(key_id >= span - rim, negative_big, spatial) + shut
+
+    blank = jnp.zeros((rim, 2 * HD), jnp.bfloat16)
+    for role in range(4):
+        for g in range(HK):
+            keyed[g, role, pl.ds(0, rim)] = blank
+            keyed[g, role, pl.ds(rim + tokens, rim)] = blank
+
+    for load in loads[3:5]:
+        load.wait()
+    hole = jnp.zeros((tiles, lane_count, HD), jnp.bfloat16)
+    for g in range(HK):
+        mixed[g, :, pl.ds(0, lane_count), pl.ds(HD, HD)] = hole
+        mixed[g, :, pl.ds(lane_count, lane_count), pl.ds(0, HD)] = hole
+        for a in range(GROUP):
+            h = g * GROUP + a
+            mixed[g, :, pl.ds(a * tile, tile), pl.ds(0, HD)] = permuted(query_ref[:, lanes(h)]).reshape(
+                tiles, tile, HD
             )
-            dot = lax.dot_general(
-                value, cot_ref[:, lanes(h)], (((1,), (1,)), ((), ())), preferred_element_type=jnp.float32
-            )
-            logit = logit * (SCALE * LOG2E) + (bias[...] + shut)
-            top = jnp.max(logit, axis=0, keepdims=True)
-            weight = jnp.exp2(logit - top)
-            probs[role, h] = weight
-            dots[role, h] = dot
-            tops[role, h] = top
-            sums[role, h] = jnp.sum(weight, axis=0, keepdims=True)
-            means[role, h] = jnp.sum(weight * dot, axis=0, keepdims=True)
+            mixed[g, :, pl.ds(lane_count + a * tile, tile), pl.ds(HD, HD)] = permuted(
+                cot_ref[:, lanes(h)]
+            ).reshape(tiles, tile, HD)
+
+    def place(role, g):
+        keyed[g, role, pl.ds(rim, tokens)] = permuted(raw[role, g])
+
+    for load in loads[5:]:
+        load.wait()
+    for g in range(HK):
+        place(0, g)
+
+    def unit(g, j):
+        first = pl.multiple_of(j * tile, tile)
+        window = keyed[g, :, pl.ds(first, span), :].reshape(4 * span, 2 * HD)
+        mix = mixed[g, j]
+        both = lax.dot_general(window, mix, (((1,), (1,)), ((), ())), preferred_element_type=jnp.float32)
+        variant = jnp.where(j == 0, 0, jnp.where(j == tiles - 1, 2, 1))
+        logit = both[:, :lane_count] * (SCALE * LOG2E) + bias[variant].reshape(4 * span, lane_count)
+        dot = both[:, lane_count:]
+        top = jnp.max(logit, axis=0, keepdims=True)
+        weight = jnp.exp2(logit - top)
+        total = jnp.sum(weight, axis=0, keepdims=True)
+        mean = jnp.sum(weight * dot, axis=0, keepdims=True) / total
+        prob = weight * (1.0 / total)
+        score = (prob * (dot - mean)).astype(jnp.bfloat16)
+        scores_low[g, j] = score
+        low = jnp.concatenate([score, prob.astype(jnp.bfloat16)], axis=1)
+        part = jnp.dot(low, mix, preferred_element_type=jnp.float32).reshape(4, span, 2 * HD)
+        begin = part[:, :tile] + held[...]
+        held[...] = part[:, tile:]
+        own_grads[g, pl.ds(first, tile)] = begin[0]
+        grads[:, g, pl.ds(first, tile)] = begin[1:].astype(jnp.bfloat16)
+
+    def queries_unit(g, j):
+        first = pl.multiple_of(j * tile, tile)
+        window = keyed[g, :, pl.ds(first, span), pl.ds(0, HD)].reshape(4 * span, HD)
+        out = jnp.dot(scores_low[g, j].T, window, preferred_element_type=jnp.float32)
+        for a in range(GROUP):
+            dq_acc[g * GROUP + a, pl.ds(first, tile)] = out[a * tile : (a + 1) * tile]
+
+    for g in range(HK):
+        for copy in send_two[g]:
+            copy.wait_recv()
+        relay[g].start()
+        place(2, g)
+        for copy in send_one[g]:
+            copy.wait_recv()
+        place(1, g)
+        relay[g].wait_recv()
+        place(3, g)
+        held[...] = jnp.zeros_like(held)
+
+        def step(j, _, g=g):
+            unit(g, j)
             return 0
 
-        lax.fori_loop(0, HQ, head, 0, unroll=4)
-
-    lag_second = jnp.where(core == 0, 3, 1)
-    lag_relay = jnp.where(core == 0, 1, 3)
-    scores(0, jnp.int32(0))
-    send_two.wait_send()
-    send_one.start()
-    send_two.wait_recv()
-    relay.start()
-    scores(2, jnp.int32(2))
-    relay.wait_recv()
-    scores(3, lag_relay)
-    send_one.wait_recv()
-    scores(1, lag_second)
-
-    def finish(h, _):
-        top = jnp.maximum(jnp.maximum(tops[0, h], tops[1, h]), jnp.maximum(tops[2, h], tops[3, h]))
-        factors = [jnp.exp2(tops[role, h] - top) for role in range(4)]
-        total = sum(factors[role] * sums[role, h] for role in range(4))
-        dot = sum(factors[role] * means[role, h] for role in range(4))
-        for role in range(4):
-            tops[role, h] = factors[role] / total
-        means[0, h] = dot / total
-        return 0
-
-    lax.fori_loop(0, HQ, finish, 0)
-
-    def gradients(role, first, store):
-        def one_group(group, _):
-            key_turned = kv[role, :, lanes(group)].T
-            key_sum = None
-            value_sum = None
-            for a in range(GROUP):
-                h = group * GROUP + a
-                prob = probs[role, h] * tops[role, h]
-                score = (prob * (dots[role, h] - means[0, h])).astype(jnp.bfloat16)
-                key_part = jnp.dot(score, query_ref[:, lanes(h)], preferred_element_type=jnp.float32)
-                value_part = jnp.dot(
-                    prob.astype(jnp.bfloat16), cot_ref[:, lanes(h)], preferred_element_type=jnp.float32
-                )
-                turned = jnp.dot(key_turned, score, preferred_element_type=jnp.float32)
-                key_sum = key_part if a == 0 else key_sum + key_part
-                value_sum = value_part if a == 0 else value_sum + value_part
-                dq_acc[h] = turned if first else dq_acc[h] + turned
-            store(group, key_sum * SCALE, value_sum)
+        lax.fori_loop(0, tiles, step, 0, unroll=UNROLL)
+        end = pl.ds(tokens, span - tile)
+        own_grads[g, end] = held[0]
+        grads[:, g, end] = held[1:].astype(jnp.bfloat16)
+        back_relay[g].start()
+        back_one[g].start()
+        back_relay[g].wait_recv()
+        grads[1, g, inner] = (
+            grads[1, g, inner].astype(jnp.float32) + arrived[2, g].astype(jnp.float32)
+        ).astype(jnp.bfloat16)
+        back_two[g].start()
+
+    for g in range(HK):
+
+        def turn_step(j, _, g=g):
+            queries_unit(g, j)
             return 0
 
-        lax.fori_loop(0, HK, one_group, 0)
-
-    def store_out(role):
-        def store(group, key_sum, value_sum):
-            grads[role, :, lanes(group)] = key_sum.astype(jnp.bfloat16)
-            grads[role, :, lanes(HK + group)] = value_sum.astype(jnp.bfloat16)
-
-        return store
-
-    back_relay = remote(3, grads.at[2], arrived.at[2], partner)
-    back_two = remote(4, grads.at[1], arrived.at[1], behind)
-    back_one = remote(5, grads.at[0], arrived.at[0], second_back)
-    gradients(3, True, store_out(2))
-    back_relay.start()
-    gradients(1, False, store_out(0))
-    back_one.start()
-
-    def store_two(group, key_sum, value_sum):
-        grads[1, :, lanes(group)] = key_sum.astype(jnp.bfloat16)
-        grads[1, :, lanes(HK + group)] = value_sum.astype(jnp.bfloat16)
-
-    gradients(2, False, store_two)
-    back_relay.wait_recv()
-    grads[1] = (grads[1].astype(jnp.float32) + arrived[2].astype(jnp.float32)).astype(jnp.bfloat16)
-    back_two.start()
-
-    def store_own(group, key_sum, value_sum):
-        kv_grads_ref[0, :, lanes(group)] = key_sum
-        kv_grads_ref[1, :, lanes(group)] = value_sum
-
-    gradients(0, False, store_own)
-
-    def query_out(h, _):
-        dq_ref[:, lanes(h)] = dq_acc[h].T * SCALE
-        return 0
-
-    lax.fori_loop(0, HQ, query_out, 0, unroll=4)
-    store_queries = pltpu.make_async_copy(dq_ref, dq_hbm, load_sem.at[7])
-    store_queries.start()
-    back_two.wait_recv()
-    back_one.wait_recv()
-    came = arrived[0].astype(jnp.float32) + arrived[1].astype(jnp.float32)
-    kv_grads_ref[0] = kv_grads_ref[0] + came[:, :heads_wide]
-    kv_grads_ref[1] = kv_grads_ref[1] + came[:, heads_wide:]
-    for copy in (send_one, relay, back_relay, back_two, back_one):
-        copy.wait_send()
-    store_queries.wait()
+        lax.fori_loop(0, tiles, turn_step, 0, unroll=UNROLL)
+
+    for h in range(HQ):
+        for r in range(rows):
+            dq_out[pl.ds(r * width, width), lanes(h)] = dq_acc[h, pl.ds(r, width, stride=rows), :] * SCALE
+
+    for g in range(HK):
+        back_one[g].wait_recv()
+        back_two[g].wait_recv()
+        came = arrived[0, g].astype(jnp.float32) + arrived[1, g].astype(jnp.float32) + own_grads[g, inner]
+        final[0, g] = came[:, :HD] * SCALE
+        final[1, g] = came[:, HD:]
+        for r in range(rows):
+            dk_out[pl.ds(r * width, width), lanes(g)] = final[0, g, pl.ds(r, width, stride=rows), :]
+            dv_out[pl.ds(r * width, width), lanes(g)] = final[1, g, pl.ds(r, width, stride=rows), :]
+    for g in range(HK):
+        for copy in send_two[g] + send_one[g] + (relay[g], back_relay[g], back_two[g], back_one[g]):
+            copy.wait_send()
+
+
+UNROLL = 8
+VL = 62 * 1024 * 1024
 
 
 def fused_body(queries, keys, values, grad_out, frame_mask, clip_frames, offsets):
@@ -455,6 +488,10 @@
     tokens = rows * width
     narrow = keys.shape[3]
     frames = lax.axis_size("tm")
+    tiles = width // TILE
+    tile = TILE * rows
+    padded = tokens + 2 * REACH * rows
+    span = tile + 2 * REACH * rows
 
     def flat(array):
         return array.reshape(tokens, array.shape[3])
@@ -465,41 +502,42 @@
     def kernel(*refs):
         fused(width, frames, *refs)
 
-    dq, kv_grads = pl.pallas_call(
+    dq, dk, dv = pl.pallas_call(
         kernel,
         out_shape=(
-            jax.ShapeDtypeStruct((tokens, wide), jnp.float32),
-            jax.ShapeDtypeStruct((2, tokens, narrow), jnp.float32),
+            pltpu.VMEM((tokens, wide), jnp.float32),
+            pltpu.VMEM((tokens, narrow), jnp.float32),
+            pltpu.VMEM((tokens, narrow), jnp.float32),
         ),
         in_specs=[hbm] * 7,
-        out_specs=(hbm, vmem),
+        out_specs=(vmem, vmem, vmem),
         scratch_shapes=[
-            pltpu.VMEM((tokens, wide), jnp.float32),
             pltpu.SMEM(frame_mask.shape, jnp.int32),
             pltpu.SMEM(clip_frames.shape, jnp.int32),
             pltpu.SMEM(offsets.shape[::-1], jnp.int32),
             pltpu.VMEM((tokens, wide), jnp.bfloat16),
             pltpu.VMEM((tokens, wide), jnp.bfloat16),
-            pltpu.VMEM((4, tokens, 2 * narrow), jnp.bfloat16),
-            pltpu.VMEM((3, tokens, 2 * narrow), jnp.bfloat16),
-            pltpu.VMEM((3, tokens, 2 * narrow), jnp.bfloat16),
-            pltpu.VMEM((tokens, tokens), jnp.float32),
-            pltpu.VMEM((4, HQ, tokens, tokens), jnp.float32),
-            pltpu.VMEM((4, HQ, tokens, tokens), jnp.float32),
-            pltpu.VMEM((4, HQ, 1, tokens), jnp.float32),
-            pltpu.VMEM((4, HQ, 1, tokens), jnp.float32),
-            pltpu.VMEM((4, HQ, 1, tokens), jnp.float32),
-            pltpu.VMEM((HQ, HD, tokens), jnp.float32),
-            pltpu.SemaphoreType.DMA((8,)),
-            pltpu.SemaphoreType.DMA((6,)),
-            pltpu.SemaphoreType.DMA((6,)),
+            pltpu.VMEM((4, HK, tokens, 2 * HD), jnp.bfloat16),
+            pltpu.VMEM((HK, 4, padded, 2 * HD), jnp.bfloat16),
+            pltpu.VMEM((HK, tiles, 2 * GROUP * tile, 2 * HD), jnp.bfloat16),
+            pltpu.VMEM((3, 4, span, GROUP * tile), jnp.float32),
+            pltpu.VMEM((4, span - tile, 2 * HD), jnp.float32),
+            pltpu.VMEM((HK, padded, 2 * HD), jnp.float32),
+            pltpu.VMEM((3, HK, padded, 2 * HD), jnp.bfloat16),
+            pltpu.VMEM((3, HK, tokens, 2 * HD), jnp.bfloat16),
+            pltpu.VMEM((HK, tiles, 4 * span, GROUP * tile), jnp.bfloat16),
+            pltpu.VMEM((HQ, tokens, HD), jnp.float32),
+            pltpu.VMEM((2, HK, tokens, HD), jnp.float32),
+            pltpu.SemaphoreType.DMA((9,)),
+            pltpu.SemaphoreType.DMA((16,)),
+            pltpu.SemaphoreType.DMA((16,)),
         ],
         compiler_params=pltpu.CompilerParams(
-            collective_id=0, has_side_effects=True, vmem_limit_bytes=63 * 1024 * 1024 - 65536
+            collective_id=0, has_side_effects=True, vmem_limit_bytes=VL
         ),
     )(frame_mask, clip_frames, offsets.T, flat(queries), flat(keys), flat(values), flat(grad_out))
     shape = (1, rows, width)
-    return dq.reshape(shape + (wide,)), kv_grads[0].reshape(shape + (narrow,)), kv_grads[1].reshape(shape + (narrow,))
+    return dq.reshape(shape + (wide,)), dk.reshape(shape + (narrow,)), dv.reshape(shape + (narrow,))
 
 
 def solution(mesh):

time: 33.9 us -> 26.4 us (0.78)
  Pallas kernels: 30.2 us -> 23.2 us
  local copies, waits for them, and re-layouts: 2.91 us -> 2.38 us
    pallas_call x1, Pallas kernels: 30.2 us -> 23.2 us  [fused_body(): pl.pallas_call(kernel, out_shape=(pltpu.VMEM((tokens, wide), jnp.float32)...]
    slice x1 -> x0, local copies, waits for them, and re-layouts: 1.94 us -> none  [fused_body(): kv_grads[1].reshape(shape + (narrow,))]
    unnamed x3, local copies, waits for them, and re-layouts: 0.97 us -> 2.38 us
where the time goes in v1:
time: 26.4 us; the launch traced here: 26.2 us
  Pallas kernels  23.2 us (88%)
  local copies, waits for them, and re-layouts  2.38 us (9%)
  between operations  0.64 us (2%)
    pallas_call x1, Pallas kernels, fused_body(): pl.pallas_call(kernel, out_shape=(pltpu.VMEM((tokens, wide), jnp.float32)...  23.2 us
    unnamed x3, local copies, waits for them, and re-layouts  2.38 us

profile of v1, /device:TPU:0, one launch (start us, length us, event | category | flops | bytes accessed | tf_op | source)
XLA Modules:
  0.0 26.2 jit_solution(16104732392544176673)
XLA Ops:
  0.6 23.2 %shard_map.94 = (f32[256,1024]{1,0:T(8,128)S(1)}, f32[256,256]{1,0:T(8,128)S(1)}, f32[256,256]{1,0:T(8,128)S(1)}) custom-call(s32[16,16]{1,0:T(8,128)} %refs_0_.1, s32[6]{0:T(128)} %refs_1_.1, s32[2,24]{1,0:T(2,128)} %bitcast.15, bf16[256,1024]{1,0:T(8,128)(2,1)} %bitcast.11, bf16[256,256]{1,0:T(8,128)(2,1)} %bitcast.13, bf16[256,256]{1,0:T(8,128)(2,1)} %bitcast.14, ...), custom_call_target="tpu_custom_call" | custom-call | tf_op jit(solution)/shard_map/pallas_call | solution.py:505
  23.9 1.0 %copy.13 = f32[1,4,64,1024]{3,2,1,0:T(8,128)} copy(f32[1,4,64,1024]{3,2,1,0:T(8,128)S(1)} %bitcast.8) | data formatting | bytes 2097152
  24.8 0.7 %copy.14 = f32[1,4,64,256]{3,2,1,0:T(8,128)} copy(f32[1,4,64,256]{3,2,1,0:T(8,128)S(1)} %bitcast.10) | data formatting | bytes 524288
  25.5 0.7 %copy.15 = f32[1,4,64,256]{3,2,1,0:T(8,128)} copy(f32[1,4,64,256]{3,2,1,0:T(8,128)S(1)} %bitcast.9) | data formatting | bytes 524288

commit v2 on v1

--- a/solution.py
+++ b/solution.py
@@ -268,7 +268,7 @@
 def fused(
     width, frames,
     mask_hbm, clip_hbm, offset_hbm, query_hbm, key_hbm, value_hbm, cot_hbm,
-    dq_out, dk_out, dv_out,
+    dq_out, dkv_out,
     mask_ref, clip_ref, offset_ref, query_ref, cot_ref, raw, keyed, mixed, bias, held, own_grads, grads, arrived,
     scores_low, dq_acc, final, load_sem, send_sem, recv_sem,
 ):
@@ -333,9 +333,8 @@
     back_one = [remote(14 + g, grads.at[0, g, inner], arrived.at[0, g], second_back) for g in range(HK)]
 
     pl.semaphore_wait(barrier, 3)
-    for g in range(HK):
-        for copy in send_two[g] + send_one[g]:
-            copy.start()
+    for copy in send_two[0] + send_one[0]:
+        copy.start()
 
     new_id = lax.broadcasted_iota(jnp.int32, (tokens, tokens), 0)
     old_id = lax.broadcasted_iota(jnp.int32, (tokens, tokens), 1)
@@ -387,6 +386,12 @@
             mixed[g, :, pl.ds(lane_count + a * tile, tile), pl.ds(HD, HD)] = permuted(
                 cot_ref[:, lanes(h)]
             ).reshape(tiles, tile, HD)
+
+    def follow(first, then):
+        for copy in first:
+            copy.wait_send()
+        for copy in then:
+            copy.start()
 
     def place(role, g):
         keyed[g, role, pl.ds(rim, tokens)] = permuted(raw[role, g])
@@ -425,7 +430,7 @@
         for a in range(GROUP):
             dq_acc[g * GROUP + a, pl.ds(first, tile)] = out[a * tile : (a + 1) * tile]
 
-    for g in range(HK):
+    def receive(g):
         for copy in send_two[g]:
             copy.wait_recv()
         relay[g].start()
@@ -435,9 +440,12 @@
         place(1, g)
         relay[g].wait_recv()
         place(3, g)
+
+
+    def work(g):
         held[...] = jnp.zeros_like(held)
 
-        def step(j, _, g=g):
+        def step(j, _):
             unit(g, j)
             return 0
 
@@ -447,11 +455,21 @@
         grads[:, g, end] = held[1:].astype(jnp.bfloat16)
         back_relay[g].start()
         back_one[g].start()
+
+    def pass_two(g):
         back_relay[g].wait_recv()
         grads[1, g, inner] = (
             grads[1, g, inner].astype(jnp.float32) + arrived[2, g].astype(jnp.float32)
         ).astype(jnp.bfloat16)
         back_two[g].start()
+
+    follow(send_two[0] + send_one[0], send_two[1] + send_one[1])
+    receive(0)
+    work(0)
+    pass_two(0)
+    receive(1)
+    work(1)
+    pass_two(1)
 
     for g in range(HK):
 
@@ -472,10 +490,12 @@
         final[0, g] = came[:, :HD] * SCALE
         final[1, g] = came[:, HD:]
         for r in range(rows):
-            dk_out[pl.ds(r * width, width), lanes(g)] = final[0, g, pl.ds(r, width, stride=rows), :]
-            dv_out[pl.ds(r * width, width), lanes(g)] = final[1, g, pl.ds(r, width, stride=rows), :]
+            dkv_out[0, pl.ds(r * width, width), lanes(g)] = final[0, g, pl.ds(r, width, stride=rows), :]
+            dkv_out[1, pl.ds(r * width, width), lanes(g)] = final[1, g, pl.ds(r, width, stride=rows), :]
+    for copy in send_two[1] + send_one[1]:
+        copy.wait_send()
     for g in range(HK):
-        for copy in send_two[g] + send_one[g] + (relay[g], back_relay[g], back_two[g], back_one[g]):
+        for copy in (relay[g], back_relay[g], back_two[g], back_one[g]):
             copy.wait_send()
 
 
@@ -502,15 +522,14 @@
     def kernel(*refs):
         fused(width, frames, *refs)
 
-    dq, dk, dv = pl.pallas_call(
+    dq, dkv = pl.pallas_call(
         kernel,
         out_shape=(
             pltpu.VMEM((tokens, wide), jnp.float32),
-            pltpu.VMEM((tokens, narrow), jnp.float32),
-            pltpu.VMEM((tokens, narrow), jnp.float32),
+            pltpu.VMEM((2, tokens, narrow), jnp.float32),
         ),
         in_specs=[hbm] * 7,
-        out_specs=(vmem, vmem, vmem),
+        out_specs=(vmem, vmem),
         scratch_shapes=[
             pltpu.SMEM(frame_mask.shape, jnp.int32),
             pltpu.SMEM(clip_frames.shape, jnp.int32),
@@ -537,7 +556,7 @@
         ),
     )(frame_mask, clip_frames, offsets.T, flat(queries), flat(keys), flat(values), flat(grad_out))
     shape = (1, rows, width)
-    return dq.reshape(shape + (wide,)), dk.reshape(shape + (narrow,)), dv.reshape(shape + (narrow,))
+    return dq.reshape(shape + (wide,)), dkv[0].reshape(shape + (narrow,)), dkv[1].reshape(shape + (narrow,))
 
 
 def solution(mesh):

time: 26.4 us -> 25.1 us (0.951)
  Pallas kernels: 23.2 us -> 22.5 us
  local copies, waits for them, and re-layouts: 2.38 us -> 1.8 us
    unnamed x3 -> x1, local copies, waits for them, and re-layouts: 2.38 us -> 0.97 us
    slice x0 -> x1, local copies, waits for them, and re-layouts: none -> 0.82 us  [fused_body(): dkv[1].reshape(shape + (narrow,))]
    pallas_call x1, Pallas kernels: 23.2 us -> 22.5 us  [fused_body(): pl.pallas_call(kernel, out_shape=(pltpu.VMEM((tokens, wide), jnp.float32)...]
where the time goes in v2:
time: 25.1 us; the launch traced here: 25 us
  Pallas kernels  22.5 us (90%)
  local copies, waits for them, and re-layouts  1.8 us (7%)
  between operations  0.64 us (3%)
    pallas_call x1, Pallas kernels, fused_body(): pl.pallas_call(kernel, out_shape=(pltpu.VMEM((tokens, wide), jnp.float32)...  22.5 us
    unnamed x1, local copies, waits for them, and re-layouts  0.97 us
    slice x1, local copies, waits for them, and re-layouts, fused_body(): dkv[1].reshape(shape + (narrow,))  0.82 us

profile of v2, /device:TPU:0, one launch (start us, length us, event | category | flops | bytes accessed | tf_op | source)
XLA Modules:
  0.0 25.0 jit_solution(8702088515044673202)
XLA Ops:
  0.6 22.5 %shard_map.94 = (f32[256,1024]{1,0:T(8,128)S(1)}, f32[2,256,256]{2,1,0:T(8,128)S(1)}) custom-call(s32[16,16]{1,0:T(8,128)} %refs_0_.1, s32[6]{0:T(128)} %refs_1_.1, s32[2,24]{1,0:T(2,128)} %bitcast.15, bf16[256,1024]{1,0:T(8,128)(2,1)} %bitcast.9, bf16[256,256]{1,0:T(8,128)(2,1)} %bitcast.13, bf16[256,256]{1,0:T(8,128)(2,1)} %bitcast.14, ...), custom_call_target="tpu_custom_call" | custom-call | tf_op jit(solution)/shard_map/pallas_call | solution.py:525
  23.2 1.0 %copy.11 = f32[1,4,64,1024]{3,2,1,0:T(8,128)} copy(f32[1,4,64,1024]{3,2,1,0:T(8,128)S(1)} %bitcast.8) | data formatting | bytes 2097152
  24.1 0.8 %fusion = (f32[1,256,256]{2,1,0:T(8,128)}, f32[1,256,256]{2,1,0:T(8,128)}) fusion(f32[2,256,256]{2,1,0:T(8,128)S(1)} %get-tuple-element.6), kind=kLoop, calls=%fused_computation | loop fusion | bytes 1048576 | tf_op jit(solution)/shard_map/slice | solution.py:559

commit v3 on v2

--- a/solution.py
+++ b/solution.py
@@ -500,7 +500,7 @@
 
 
 UNROLL = 8
-VL = 62 * 1024 * 1024
+VL = 40 * 1024 * 1024
 
 
 def fused_body(queries, keys, values, grad_out, frame_mask, clip_frames, offsets):
@@ -554,9 +554,35 @@
         compiler_params=pltpu.CompilerParams(
             collective_id=0, has_side_effects=True, vmem_limit_bytes=VL
         ),
-    )(frame_mask, clip_frames, offsets.T, flat(queries), flat(keys), flat(values), flat(grad_out))
+    )(*[
+        pltpu.with_memory_space_constraint(operand, pltpu.HBM)
+        for operand in (
+            frame_mask, clip_frames, offsets.T, flat(queries), flat(keys), flat(values), flat(grad_out)
+        )
+    ])
+    def ship(dq_ref, dkv_ref, dq_out, dk_out, dv_out, sem):
+        pairs = ((dq_ref, dq_out), (dkv_ref.at[0], dk_out), (dkv_ref.at[1], dv_out))
+        copies = [pltpu.make_async_copy(pair[0], pair[1], sem.at[i]) for i, pair in enumerate(pairs)]
+        for copy in copies:
+            copy.start()
+        for copy in copies:
+            copy.wait()
+
+    dq, dk, dv = pl.pallas_call(
+        ship,
+        out_shape=(
+            jax.ShapeDtypeStruct((tokens, wide), jnp.float32),
+            jax.ShapeDtypeStruct((tokens, narrow), jnp.float32),
+            jax.ShapeDtypeStruct((tokens, narrow), jnp.float32),
+        ),
+        in_specs=[vmem] * 2,
+        out_specs=[hbm] * 3,
+        scratch_shapes=[pltpu.SemaphoreType.DMA((3,))],
+        compiler_params=pltpu.CompilerParams(vmem_limit_bytes=4 * 1024 * 1024),
+        name="ship",
+    )(*[pltpu.with_memory_space_constraint(part, pltpu.VMEM) for part in (dq, dkv)])
     shape = (1, rows, width)
-    return dq.reshape(shape + (wide,)), dkv[0].reshape(shape + (narrow,)), dkv[1].reshape(shape + (narrow,))
+    return dq.reshape(shape + (wide,)), dk.reshape(shape + (narrow,)), dv.reshape(shape + (narrow,))
 
 
 def solution(mesh):

time: 25.1 us -> 24.5 us (0.976)
  local copies, waits for them, and re-layouts: 1.8 us -> 0 us
  Pallas kernels: 22.5 us -> 23.7 us
    pallas_call x0 -> x1, Pallas kernels: none -> 1.16 us  [fused_body(): pl.pallas_call(ship, out_shape=(jax.ShapeDtypeStruct((tokens, wide), jnp....]
    unnamed x1 -> x0, local copies, waits for them, and re-layouts: 0.97 us -> none
    slice x1 -> x0, local copies, waits for them, and re-layouts: 0.82 us -> none  [fused_body(): dkv[1].reshape(shape + (narrow,))]
where the time goes in v3:
time: 24.5 us; the launch traced here: 24.3 us
  Pallas kernels  23.7 us (97%)
  between operations  0.64 us (3%)
    pallas_call x1, Pallas kernels, fused_body(): pl.pallas_call(kernel, out_shape=(pltpu.VMEM((tokens, wide), jnp.float32)...  22.5 us
    pallas_call x1, Pallas kernels, fused_body(): pl.pallas_call(ship, out_shape=(jax.ShapeDtypeStruct((tokens, wide), jnp....  1.16 us

profile of v3, /device:TPU:0, one launch (start us, length us, event | category | flops | bytes accessed | tf_op | source)
XLA Modules:
  0.0 24.3 jit_solution(7117089253020169822)
XLA Ops:
  0.6 22.5 %shard_map.94 = (f32[256,1024]{1,0:T(8,128)S(1)}, f32[2,256,256]{2,1,0:T(8,128)S(1)}) custom-call(s32[16,16]{1,0:T(8,128)} %refs_0_.1, s32[6]{0:T(128)} %refs_1_.1, s32[2,24]{1,0:T(2,128)} %bitcast.12, bf16[256,1024]{1,0:T(8,128)(2,1)} %bitcast.8, bf16[256,256]{1,0:T(8,128)(2,1)} %bitcast.10, bf16[256,256]{1,0:T(8,128)(2,1)} %bitcast.11, ...), custom_call_target="tpu_custom_call" | custom-call | tf_op jit(solution)/shard_map/pallas_call | solution.py:525
  23.2 1.2 %ship.1 = (f32[256,1024]{1,0:T(8,128)}, f32[256,256]{1,0:T(8,128)}, f32[256,256]{1,0:T(8,128)}) custom-call(f32[256,1024]{1,0:T(8,128)S(1)} %get-tuple-element.8.dq_ref, f32[2,256,256]{2,1,0:T(8,128)S(1)} %get-tuple-element.9.dkv_ref), custom_call_target="tpu_custom_call" | custom-call | tf_op jit(solution)/shard_map/ship/pallas_call | solution.py:571

commit v4 on v3

--- a/solution.py
+++ b/solution.py
@@ -319,6 +319,8 @@
         )
 
     def outward(slot, role, g, peer):
+        if g in STAGED:
+            return (remote(slot, raw.at[0, g], raw.at[role, g], peer),)
         return (
             remote(slot, key_hbm.at[:, lanes(g)], raw.at[role, g, :, pl.ds(0, HD)], peer),
             remote(slot + 1, value_hbm.at[:, lanes(g)], raw.at[role, g, :, pl.ds(HD, HD)], peer),
@@ -333,8 +335,18 @@
     back_one = [remote(14 + g, grads.at[0, g, inner], arrived.at[0, g], second_back) for g in range(HK)]
 
     pl.semaphore_wait(barrier, 3)
+    odd_last = lax.rem(own, 4) == 3
     for copy in send_two[0] + send_one[0]:
         copy.start()
+
+    for load in loads[7:]:
+        load.wait()
+
+    @pl.when(jnp.logical_not(odd_last))
+    def _():
+        for copy in send_one[1]:
+            copy.start()
+
 
     new_id = lax.broadcasted_iota(jnp.int32, (tokens, tokens), 0)
     old_id = lax.broadcasted_iota(jnp.int32, (tokens, tokens), 1)
@@ -396,7 +408,7 @@
     def place(role, g):
         keyed[g, role, pl.ds(rim, tokens)] = permuted(raw[role, g])
 
-    for load in loads[5:]:
+    for load in loads[5:7]:
         load.wait()
     for g in range(HK):
         place(0, g)
@@ -463,7 +475,13 @@
         ).astype(jnp.bfloat16)
         back_two[g].start()
 
-    follow(send_two[0] + send_one[0], send_two[1] + send_one[1])
+    follow(send_two[0], send_two[1])
+    follow(send_one[0], ())
+
+    @pl.when(odd_last)
+    def _():
+        follow((), send_one[1])
+
     receive(0)
     work(0)
     pass_two(0)
@@ -500,6 +518,7 @@
 
 
 UNROLL = 8
+STAGED = (1,)
 VL = 40 * 1024 * 1024
 
 

time: 24.5 us -> 24.2 us (0.988)
  Pallas kernels: 23.7 us -> 23.4 us
    pallas_call x1, Pallas kernels: 22.5 us -> 22.3 us  [fused_body(): pl.pallas_call(kernel, out_shape=(pltpu.VMEM((tokens, wide), jnp.float32)...]
where the time goes in v4:
time: 24.2 us; the launch traced here: 24.1 us
  Pallas kernels  23.4 us (97%)
  between operations  0.64 us (3%)
    pallas_call x1, Pallas kernels, fused_body(): pl.pallas_call(kernel, out_shape=(pltpu.VMEM((tokens, wide), jnp.float32)...  22.3 us
    pallas_call x1, Pallas kernels, fused_body(): pl.pallas_call(ship, out_shape=(jax.ShapeDtypeStruct((tokens, wide), jnp....  1.16 us

profile of v4, /device:TPU:0, one launch (start us, length us, event | category | flops | bytes accessed | tf_op | source)
XLA Modules:
  0.0 24.1 jit_solution(10732590544436534269)
XLA Ops:
  0.6 22.3 %shard_map.94 = (f32[256,1024]{1,0:T(8,128)S(1)}, f32[2,256,256]{2,1,0:T(8,128)S(1)}) custom-call(s32[16,16]{1,0:T(8,128)} %refs_0_.1, s32[6]{0:T(128)} %refs_1_.1, s32[2,24]{1,0:T(2,128)} %bitcast.12, bf16[256,1024]{1,0:T(8,128)(2,1)} %bitcast.8, bf16[256,256]{1,0:T(8,128)(2,1)} %bitcast.10, bf16[256,256]{1,0:T(8,128)(2,1)} %bitcast.11, ...), custom_call_target="tpu_custom_call" | custom-call | tf_op jit(solution)/shard_map/pallas_call | solution.py:544
  22.9 1.2 %ship.1 = (f32[256,1024]{1,0:T(8,128)}, f32[256,256]{1,0:T(8,128)}, f32[256,256]{1,0:T(8,128)}) custom-call(f32[256,1024]{1,0:T(8,128)S(1)} %get-tuple-element.8.dq_ref, f32[2,256,256]{2,1,0:T(8,128)S(1)} %get-tuple-element.9.dkv_ref), custom_call_target="tpu_custom_call" | custom-call | tf_op jit(solution)/shard_map/ship/pallas_call | solution.py:590

commit v5 on v4

--- a/solution.py
+++ b/solution.py
@@ -307,7 +307,7 @@
     second_back = device(jnp.where(core == 0, frames - 3, frames - 1))
 
     barrier = pltpu.get_barrier_semaphore()
-    for peer in (partner, behind, third):
+    for peer in (behind, third):
         pl.semaphore_signal(barrier, inc=1, device_id=peer, device_id_type=MESH)
     for load in loads:
         load.start()
@@ -334,7 +334,7 @@
     back_two = [remote(12 + g, grads.at[1, g, inner], arrived.at[1, g], behind) for g in range(HK)]
     back_one = [remote(14 + g, grads.at[0, g, inner], arrived.at[0, g], second_back) for g in range(HK)]
 
-    pl.semaphore_wait(barrier, 3)
+    pl.semaphore_wait(barrier, 2)
     odd_last = lax.rem(own, 4) == 3
     for copy in send_two[0] + send_one[0]:
         copy.start()
@@ -443,16 +443,24 @@
             dq_acc[g * GROUP + a, pl.ds(first, tile)] = out[a * tile : (a + 1) * tile]
 
     def receive(g):
+        @pl.when(core == 1)
+        def _():
+            for copy in send_one[g]:
+                copy.wait_recv()
+
         for copy in send_two[g]:
             copy.wait_recv()
         relay[g].start()
         place(2, g)
-        for copy in send_one[g]:
-            copy.wait_recv()
+
+        @pl.when(core == 0)
+        def _():
+            for copy in send_one[g]:
+                copy.wait_recv()
+
         place(1, g)
         relay[g].wait_recv()
         place(3, g)
-
 
     def work(g):
         held[...] = jnp.zeros_like(held)
@@ -476,11 +484,12 @@
         back_two[g].start()
 
     follow(send_two[0], send_two[1])
-    follow(send_one[0], ())
 
     @pl.when(odd_last)
     def _():
         follow((), send_one[1])
+
+    follow(send_one[0], ())
 
     receive(0)
     work(0)

time: 24.2 us -> 24 us (level)
  no operation moved by 1% of the time
where the time goes in v5:
time: 24 us; the launch traced here: 23.9 us
  Pallas kernels  23.2 us (97%)
  between operations  0.64 us (3%)
    pallas_call x1, Pallas kernels, fused_body(): pl.pallas_call(kernel, out_shape=(pltpu.VMEM((tokens, wide), jnp.float32)...  22.1 us
    pallas_call x1, Pallas kernels, fused_body(): pl.pallas_call(ship, out_shape=(jax.ShapeDtypeStruct((tokens, wide), jnp....  1.16 us

profile of v5, /device:TPU:0, one launch (start us, length us, event | category | flops | bytes accessed | tf_op | source)
XLA Modules:
  0.0 23.9 jit_solution(15253537980588529320)
XLA Ops:
  0.6 22.1 %shard_map.94 = (f32[256,1024]{1,0:T(8,128)S(1)}, f32[2,256,256]{2,1,0:T(8,128)S(1)}) custom-call(s32[16,16]{1,0:T(8,128)} %refs_0_.1, s32[6]{0:T(128)} %refs_1_.1, s32[2,24]{1,0:T(2,128)} %bitcast.12, bf16[256,1024]{1,0:T(8,128)(2,1)} %bitcast.8, bf16[256,256]{1,0:T(8,128)(2,1)} %bitcast.10, bf16[256,256]{1,0:T(8,128)(2,1)} %bitcast.11, ...), custom_call_target="tpu_custom_call" | custom-call | tf_op jit(solution)/shard_map/pallas_call | solution.py:553
  22.7 1.2 %ship.1 = (f32[256,1024]{1,0:T(8,128)}, f32[256,256]{1,0:T(8,128)}, f32[256,256]{1,0:T(8,128)}) custom-call(f32[256,1024]{1,0:T(8,128)S(1)} %get-tuple-element.8.dq_ref, f32[2,256,256]{2,1,0:T(8,128)S(1)} %get-tuple-element.9.dkv_ref), custom_call_target="tpu_custom_call" | custom-call | tf_op jit(solution)/shard_map/ship/pallas_call | solution.py:599

commit v6 on v5

--- a/solution.py
+++ b/solution.py
@@ -309,8 +309,6 @@
     barrier = pltpu.get_barrier_semaphore()
     for peer in (behind, third):
         pl.semaphore_signal(barrier, inc=1, device_id=peer, device_id_type=MESH)
-    for load in loads:
-        load.start()
 
     def remote(index, source, target, peer):
         return pltpu.make_async_remote_copy(
@@ -338,6 +336,8 @@
     odd_last = lax.rem(own, 4) == 3
     for copy in send_two[0] + send_one[0]:
         copy.start()
+    for load in loads[7:] + loads[:7]:
+        load.start()
 
     for load in loads[7:]:
         load.wait()

time: 24 us -> 24 us (level)
  no operation moved by 1% of the time
where the time goes in v6:
time: 24 us; the launch traced here: 23.9 us
  Pallas kernels  23.2 us (97%)
  between operations  0.64 us (3%)
    pallas_call x1, Pallas kernels, fused_body(): pl.pallas_call(kernel, out_shape=(pltpu.VMEM((tokens, wide), jnp.float32)...  22.1 us
    pallas_call x1, Pallas kernels, fused_body(): pl.pallas_call(ship, out_shape=(jax.ShapeDtypeStruct((tokens, wide), jnp....  1.16 us

profile of v6, /device:TPU:0, one launch (start us, length us, event | category | flops | bytes accessed | tf_op | source)
XLA Modules:
  0.0 23.9 jit_solution(9036631628687918398)
XLA Ops:
  0.6 22.1 %shard_map.94 = (f32[256,1024]{1,0:T(8,128)S(1)}, f32[2,256,256]{2,1,0:T(8,128)S(1)}) custom-call(s32[16,16]{1,0:T(8,128)} %refs_0_.1, s32[6]{0:T(128)} %refs_1_.1, s32[2,24]{1,0:T(2,128)} %bitcast.12, bf16[256,1024]{1,0:T(8,128)(2,1)} %bitcast.8, bf16[256,256]{1,0:T(8,128)(2,1)} %bitcast.10, bf16[256,256]{1,0:T(8,128)(2,1)} %bitcast.11, ...), custom_call_target="tpu_custom_call" | custom-call | tf_op jit(solution)/shard_map/pallas_call | solution.py:553
  22.7 1.2 %ship.1 = (f32[256,1024]{1,0:T(8,128)}, f32[256,256]{1,0:T(8,128)}, f32[256,256]{1,0:T(8,128)}) custom-call(f32[256,1024]{1,0:T(8,128)S(1)} %get-tuple-element.8.dq_ref, f32[2,256,256]{2,1,0:T(8,128)S(1)} %get-tuple-element.9.dkv_ref), custom_call_target="tpu_custom_call" | custom-call | tf_op jit(solution)/shard_map/ship/pallas_call | solution.py:599

commit v7 on v6

--- a/solution.py
+++ b/solution.py
@@ -269,7 +269,7 @@
     width, frames,
     mask_hbm, clip_hbm, offset_hbm, query_hbm, key_hbm, value_hbm, cot_hbm,
     dq_out, dkv_out,
-    mask_ref, clip_ref, offset_ref, query_ref, cot_ref, raw, keyed, mixed, bias, held, own_grads, grads, arrived,
+    mask_ref, clip_ref, offset_ref, query_ref, cot_ref, raw, keyed, mixed, bias, own_grads, grads, arrived,
     scores_low, dq_acc, final, load_sem, send_sem, recv_sem,
 ):
     tokens = query_ref.shape[0]
@@ -413,12 +413,12 @@
     for g in range(HK):
         place(0, g)
 
-    def unit(g, j):
-        first = pl.multiple_of(j * tile, tile)
+    def unit(g, j, held):
+        first = j * tile
         window = keyed[g, :, pl.ds(first, span), :].reshape(4 * span, 2 * HD)
         mix = mixed[g, j]
         both = lax.dot_general(window, mix, (((1,), (1,)), ((), ())), preferred_element_type=jnp.float32)
-        variant = jnp.where(j == 0, 0, jnp.where(j == tiles - 1, 2, 1))
+        variant = 0 if j == 0 else 2 if j == tiles - 1 else 1
         logit = both[:, :lane_count] * (SCALE * LOG2E) + bias[variant].reshape(4 * span, lane_count)
         dot = both[:, lane_count:]
         top = jnp.max(logit, axis=0, keepdims=True)
@@ -430,10 +430,10 @@
         scores_low[g, j] = score
         low = jnp.concatenate([score, prob.astype(jnp.bfloat16)], axis=1)
         part = jnp.dot(low, mix, preferred_element_type=jnp.float32).reshape(4, span, 2 * HD)
-        begin = part[:, :tile] + held[...]
-        held[...] = part[:, tile:]
+        begin = part[:, :tile] if held is None else part[:, :tile] + held
         own_grads[g, pl.ds(first, tile)] = begin[0]
         grads[:, g, pl.ds(first, tile)] = begin[1:].astype(jnp.bfloat16)
+        return part[:, tile:]
 
     def queries_unit(g, j):
         first = pl.multiple_of(j * tile, tile)
@@ -463,13 +463,9 @@
         place(3, g)
 
     def work(g):
-        held[...] = jnp.zeros_like(held)
-
-        def step(j, _):
-            unit(g, j)
-            return 0
-
-        lax.fori_loop(0, tiles, step, 0, unroll=UNROLL)
+        held = None
+        for j in range(tiles):
+            held = unit(g, j, held)
         end = pl.ds(tokens, span - tile)
         own_grads[g, end] = held[0]
         grads[:, g, end] = held[1:].astype(jnp.bfloat16)
@@ -568,7 +564,6 @@
             pltpu.VMEM((HK, 4, padded, 2 * HD), jnp.bfloat16),
             pltpu.VMEM((HK, tiles, 2 * GROUP * tile, 2 * HD), jnp.bfloat16),
             pltpu.VMEM((3, 4, span, GROUP * tile), jnp.float32),
-            pltpu.VMEM((4, span - tile, 2 * HD), jnp.float32),
             pltpu.VMEM((HK, padded, 2 * HD), jnp.float32),
             pltpu.VMEM((3, HK, padded, 2 * HD), jnp.bfloat16),
             pltpu.VMEM((3, HK, tokens, 2 * HD), jnp.bfloat16),

time: 24 us -> 24 us (level)
  no operation moved by 1% of the time
where the time goes in v7:
time: 24 us; the launch traced here: 23.9 us
  Pallas kernels  23.2 us (97%)
  between operations  0.64 us (3%)
    pallas_call x1, Pallas kernels, fused_body(): pl.pallas_call(kernel, out_shape=(pltpu.VMEM((tokens, wide), jnp.float32)...  22.1 us
    pallas_call x1, Pallas kernels, fused_body(): pl.pallas_call(ship, out_shape=(jax.ShapeDtypeStruct((tokens, wide), jnp....  1.16 us

profile of v7, /device:TPU:0, one launch (start us, length us, event | category | flops | bytes accessed | tf_op | source)
XLA Modules:
  0.0 23.9 jit_solution(6484180384016498776)
XLA Ops:
  0.6 22.1 %shard_map.94 = (f32[256,1024]{1,0:T(8,128)S(1)}, f32[2,256,256]{2,1,0:T(8,128)S(1)}) custom-call(s32[16,16]{1,0:T(8,128)} %refs_0_.1, s32[6]{0:T(128)} %refs_1_.1, s32[2,24]{1,0:T(2,128)} %bitcast.12, bf16[256,1024]{1,0:T(8,128)(2,1)} %bitcast.8, bf16[256,256]{1,0:T(8,128)(2,1)} %bitcast.10, bf16[256,256]{1,0:T(8,128)(2,1)} %bitcast.11, ...), custom_call_target="tpu_custom_call" | custom-call | tf_op jit(solution)/shard_map/pallas_call | solution.py:549
  22.7 1.2 %ship.1 = (f32[256,1024]{1,0:T(8,128)}, f32[256,256]{1,0:T(8,128)}, f32[256,256]{1,0:T(8,128)}) custom-call(f32[256,1024]{1,0:T(8,128)S(1)} %get-tuple-element.8.dq_ref, f32[2,256,256]{2,1,0:T(8,128)S(1)} %get-tuple-element.9.dkv_ref), custom_call_target="tpu_custom_call" | custom-call | tf_op jit(solution)/shard_map/ship/pallas_call | solution.py:594
